TPU v7x, 32 devices: a whole 2x2x4 slice. The times are simulated.
32 devices in a mesh: row: 8 (over y, x, core), col: 4 (over z).
Axes of the slice: x: 2, y: 2, z: 4, core: 2. Of those that a mesh axis runs over, the one named last changes fastest.
Arguments:
- src_latent: bfloat16 [32, 32768], P(None, 'row'), may hold values from -6 to 6
- tgt_latent: bfloat16 [32, 8192], P(None, 'col'), may hold values from -6 to 6
- g_start: float32 [8192], P('col'), may hold values from -1.5 to 1.5
- pairs: int32 [8, 4, 8, 2], P('row', 'col'), may hold values from 0 to 7, as said below
- counts: int32 [8, 4], P('row', 'col'), may hold values from 1 to 8, as said below
Outputs:
- f_new: float32 [32768], P('row')
- g_new: float32 [8192], P('col')
- bary: float32 [32, 32768], P(None, 'row')
Inputs may be any that keep to these rules, and one draw needn't show every extreme that they name: Within one device's 8 slots all pairs are distinct; entry 0 is below 8 and entry 1 below 4. Every source block and every target block appears among the live slots of some device. `counts`: some device has exactly 8 live slots in every draw.
All inputs are finite; a program needn't handle non-finite values.
Results may differ from a plain program's by a relative error of at most 0.0012.
Values sent between devices are 32-bit elements; how exact they have to be, the bound alone decides.
A program may use at most 64 MiB of HBM per device.

v0:
```python
import functools
import math

import jax
import jax.numpy as jnp
from jax import lax
from jax.experimental import pallas as pl
from jax.experimental.pallas import tpu as pltpu
from jax.sharding import PartitionSpec as P

BLOCK = 512
HALF = 256
SUMS = 16
RUN = 64

epsilon = 0.01
very_low = -1e30
log2e = 1.0 / math.log(2.0)
MESH = pl.DeviceIdType.MESH


def dot(a, b, a_dim, b_dim):
    return lax.dot_general(
        a, b, (((a_dim,), (b_dim,)), ((), ())), preferred_element_type=jnp.float32
    )


def three(v):
    hi = v.astype(jnp.bfloat16).astype(jnp.float32)
    rest = v - hi
    mid = rest.astype(jnp.bfloat16).astype(jnp.float32)
    return hi, mid, rest - mid


def tail(rows, first, second):
    row = lax.broadcasted_iota(jnp.int32, (8, BLOCK), 0)
    out = jnp.zeros((8, BLOCK), jnp.float32)
    for start, value in ((0, first), (3, second)):
        if isinstance(value, tuple):
            for k in range(3):
                out = jnp.where(row == start + k, value[k], out)
        elif value:
            out = jnp.where((row >= start) & (row < start + 3), value, out)
    out = jnp.concatenate([out, jnp.zeros((rows - 8, BLOCK), jnp.float32)], axis=0)
    return out.astype(jnp.bfloat16)


def depth_of(width):
    return -(-(3 * width + 16) // 128) * 128


def scaled_rows(x, scale):
    return [part.astype(jnp.bfloat16) for part in three(x.astype(jnp.float32) * scale)]


def over_rows(op, x):
    while x.shape[0] > 8:
        ways = 4 if x.shape[0] % 32 == 0 else 2
        n = x.shape[0] // ways
        parts = [x[k * n : (k + 1) * n] for k in range(ways)]
        while len(parts) > 1:
            parts = [op(a, b) for a, b in zip(parts[::2], parts[1::2])]
        x = parts[0]
    return (jnp.max if op is jnp.maximum else jnp.sum)(x, axis=0, keepdims=True)


def put_scores(buf, lhs, rhs_ref, block):
    for h in range(BLOCK // HALF):
        at = slice(h * HALF, (h + 1) * HALF)
        buf[:, at] = dot(lhs, rhs_ref[block, :, at], 1, 0)


def column_top(buf, at):
    top = buf[0:RUN, at]
    for k in range(RUN, BLOCK, RUN):
        top = jnp.maximum(top, buf[k : k + RUN, at])
    return over_rows(jnp.maximum, top)


def column_lse(buf):
    out = []
    for h in range(BLOCK // HALF):
        at = slice(h * HALF, (h + 1) * HALF)
        top = column_top(buf, at)
        total = jnp.zeros((RUN, HALF), jnp.float32)
        for k in range(0, BLOCK, RUN):
            total = total + jnp.exp2(buf[k : k + RUN, at] - top)
        out.append(top + jnp.log(over_rows(jnp.add, total)) * log2e)
    return jnp.concatenate(out, axis=1)


def merge_slots(lse, ids, block):
    own = ids == block
    top = jnp.max(jnp.where(own, lse, very_low), axis=0, keepdims=True)
    total = jnp.sum(jnp.where(own, jnp.exp2(lse - top), 0.0), axis=0, keepdims=True)
    return jnp.where(total > 0.0, top + jnp.log(jnp.maximum(total, 1e-30)) * log2e, very_low)


def merge_devices(ref, n):
    top = lax.fori_loop(1, n, lambda c, t: jnp.maximum(t, ref[c]), ref[0])
    total = lax.fori_loop(
        0, n, lambda c, t: t + jnp.exp2(ref[c] - top), jnp.zeros(top.shape, jnp.float32)
    )
    return top + jnp.log(total) * log2e


def potentials_kernel(
    n_row, n_col, sb, tb, slots, width,
    x_hbm, y_hbm, g_hbm, pairs_hbm, counts_ref,
    lse_f_ref, all_g_ref, all_y_ref, all_meta_ref,
    x_ref, y_ref, g_ref, pairs_ref, x_aug, y_aug, y_flip, y_wide, slot_lse, from_col, from_row, meta,
    meta_send, meta_recv, f_send, f_recv, g_send, g_recv, h_send, h_recv,
    y_send, y_recv, x_send, x_recv, z_send, z_recv, local_sem, *bufs,
):
    row = lax.axis_index("row")
    col = lax.axis_index("col")
    low = lax.rem(row, 2)
    high = lax.rem(row, 4) // 2
    across = row + 2 - 4 * high
    sibling = row + 1 - 2 * low
    quarter = width // 4

    def rows_of(high, low):
        return pl.ds(pl.multiple_of((2 * high + low) * quarter, quarter), quarter)

    deep = 3 * width
    extra = depth_of(width) - deep

    get_y = pltpu.make_async_copy(y_hbm, y_ref, local_sem.at[2])
    get_y.start()
    get_x = pltpu.make_async_copy(x_hbm, x_ref, local_sem.at[3])
    get_x.start()

    get_g = pltpu.make_async_copy(g_hbm, g_ref, local_sem.at[4])
    get_g.start()
    get_pairs = pltpu.make_async_copy(pairs_hbm, pairs_ref, local_sem.at[5])
    get_pairs.start()

    barrier = pltpu.get_barrier_semaphore()

    def over(n, me, do):
        def step(d, carry):
            do(lax.rem(me + d, n))
            return carry

        lax.fori_loop(1, n, step, 0)

    over(n_col, col, lambda c: pl.semaphore_signal(
        barrier, inc=1, device_id=(row, c), device_id_type=MESH))
    over(n_row, row, lambda r: pl.semaphore_signal(
        barrier, inc=1, device_id=(r, col), device_id_type=MESH))

    def to_col(src, dst, send, recv, c):
        return pltpu.make_async_remote_copy(
            src_ref=src, dst_ref=dst.at[col], send_sem=send.at[c], recv_sem=recv.at[col],
            device_id=(row, c), device_id_type=MESH)

    def from_col_of(dst, send, recv, c):
        return pltpu.make_async_remote_copy(
            src_ref=dst.at[c], dst_ref=dst.at[c], send_sem=send.at[c], recv_sem=recv.at[c],
            device_id=(row, c), device_id_type=MESH)

    get_pairs.wait()
    count = counts_ref[0, 0]
    lane = lax.broadcasted_iota(jnp.int32, (1, 128), 1)
    slot = lax.broadcasted_iota(jnp.int32, (slots, BLOCK), 0)
    ids_s = jnp.full((slots, BLOCK), -1, jnp.int32)
    ids_t = jnp.full((slots, BLOCK), -1, jnp.int32)
    packed = jnp.where(lane == 2 * slots, count, 0)
    for p in range(slots):
        ids_s = jnp.where(slot == p, pairs_ref[0, 0, 0, p], ids_s)
        ids_t = jnp.where(slot == p, pairs_ref[0, 0, 1, p], ids_t)
        packed = jnp.where(lane == 2 * p, pairs_ref[0, 0, 0, p], packed)
        packed = jnp.where(lane == 2 * p + 1, pairs_ref[0, 0, 1, p], packed)
    ids_s = jnp.where(slot < count, ids_s, -1)
    ids_t = jnp.where(slot < count, ids_t, -1)
    meta[...] = packed

    def prepare_x(s, carry):
        off = pl.multiple_of(s * BLOCK, BLOCK)
        x = x_ref[:, pl.ds(off, BLOCK)]
        for k, part in enumerate(scaled_rows(x, 2.0 * log2e / (width * epsilon))):
            x_aug[s, k * width : (k + 1) * width, :] = part
        x_aug[s, deep:, :] = tail(extra, 0.0, 1.0)
        return carry

    def prepare_y(t, carry):
        off = pl.multiple_of(t * BLOCK, BLOCK)
        y = y_ref[:, pl.ds(off, BLOCK)]
        yf = y.astype(jnp.float32)
        y_wide[:, pl.ds(off, BLOCK)] = yf
        for k in range(3):
            y_aug[t, k * width : (k + 1) * width, :] = y
        sq = jnp.sum(yf * yf, axis=0, keepdims=True)
        v = (g_ref[:, pl.ds(off, BLOCK)] - sq * (1.0 / width)) * (log2e / epsilon)
        y_aug[t, deep:, :] = tail(extra, 1.0, three(v))
        y_flip[t] = y_aug[t].T
        return carry

    get_y.wait()
    get_g.wait()
    lax.fori_loop(0, tb, prepare_y, 0)
    def y_copy(source, c):
        return pltpu.make_async_remote_copy(
            src_ref=y_wide.at[rows_of(high, low)],
            dst_ref=all_y_ref.at[source, rows_of(high, low)],
            send_sem=y_send.at[c], recv_sem=y_recv.at[source],
            device_id=(row, c), device_id_type=MESH)

    pl.semaphore_wait(barrier, n_col + n_row - 2)
    over(n_col, col, lambda c: y_copy(col, c).start())
    over(n_col, col, lambda c: to_col(meta, all_meta_ref, meta_send, meta_recv, c).start())

    local_y = pltpu.make_async_copy(y_wide, all_y_ref.at[col], local_sem.at[0])
    local_y.start()
    local_meta = pltpu.make_async_copy(meta, all_meta_ref.at[col], local_sem.at[1])
    local_meta.start()

    get_x.wait()
    lax.fori_loop(0, sb, prepare_x, 0)

    group = math.gcd(slots, 4)

    def in_turn(put, q):
        put(0)
        for k in range(group):
            if k + 1 < group:
                put(k + 1)
            slot_lse[pl.ds(q * group + k, 1), :] = column_lse(bufs[k])

    def source_step(q, carry):
        def put(k):
            p = q * group + k
            put_scores(bufs[k], y_flip[pairs_ref[0, 0, 1, p]], x_aug, pairs_ref[0, 0, 0, p])

        in_turn(put, q)
        return carry

    lax.fori_loop(0, slots // group, source_step, 0)
    lse = slot_lse[...]
    for s in range(sb):
        lse_f_ref[s : s + 1, :] = merge_slots(lse, ids_s, s)
    from_col[col] = lse_f_ref[...]

    over(n_col, col, lambda c: to_col(lse_f_ref, from_col, f_send, f_recv, c).start())
    over(n_col, col, lambda c: from_col_of(from_col, f_send, f_recv, c).wait_recv())

    def x_copy(source, high):
        return pltpu.make_async_remote_copy(
            src_ref=all_y_ref.at[source, rows_of(high, low)],
            dst_ref=all_y_ref.at[source, rows_of(high, low)],
            send_sem=x_send.at[source], recv_sem=x_recv.at[source],
            device_id=(across, col), device_id_type=MESH)

    def pass_across(c):
        y_copy(c, c).wait_recv()
        x_copy(c, high).start()

    over(n_col, col, pass_across)
    over(n_col, col, lambda c: to_col(lse_f_ref, from_col, f_send, f_recv, c).wait_send())

    merged = merge_devices(from_col, n_col)
    lse_f_ref[...] = merged
    for s in range(sb):
        u = -math.log2(sb * BLOCK * n_row) - merged[s : s + 1, :]
        x_aug[s, deep:, :] = tail(extra, three(u), 0.0)

    def target_step(q, carry):
        def put(k):
            p = q * group + k
            put_scores(bufs[k], x_aug[pairs_ref[0, 0, 0, p]].T, y_aug, pairs_ref[0, 0, 1, p])

        in_turn(put, q)
        return carry

    lax.fori_loop(0, slots // group, target_step, 0)
    lse = slot_lse[...]
    for t in range(tb):
        from_row[row, t : t + 1, :] = merge_slots(lse, ids_t, t)

    def g_copy(source, r):
        return pltpu.make_async_remote_copy(
            src_ref=from_row.at[source], dst_ref=from_row.at[source],
            send_sem=g_send.at[r], recv_sem=g_recv.at[source],
            device_id=(r, col), device_id_type=MESH)

    over(n_row, row, lambda r: g_copy(row, r).start())

    def z_copy(source, k, high, low):
        return pltpu.make_async_remote_copy(
            src_ref=all_y_ref.at[source, rows_of(high, low)],
            dst_ref=all_y_ref.at[source, rows_of(high, low)],
            send_sem=z_send.at[k, source], recv_sem=z_recv.at[k, source],
            device_id=(sibling, col), device_id_type=MESH)

    def pass_to_sibling(c):
        x_copy(c, 1 - high).wait_recv()
        z_copy(c, 0, high, low).start()
        z_copy(c, 1, 1 - high, low).start()

    def wait_from_sibling(c):
        z_copy(c, 0, high, 1 - low).wait_recv()
        z_copy(c, 1, 1 - high, 1 - low).wait_recv()

    def wait_to_sibling(c):
        z_copy(c, 0, high, low).wait_send()
        z_copy(c, 1, 1 - high, low).wait_send()

    over(n_col, col, pass_to_sibling)
    over(n_row, row, lambda r: g_copy(r, r).wait_recv())
    all_g_ref[col] = merge_devices(from_row, n_row)

    def h_copy(source, c):
        return pltpu.make_async_remote_copy(
            src_ref=all_g_ref.at[source], dst_ref=all_g_ref.at[source],
            send_sem=h_send.at[c], recv_sem=h_recv.at[source],
            device_id=(row, c), device_id_type=MESH)

    over(n_col, col, lambda c: h_copy(col, c).start())

    over(n_col, col, lambda c: h_copy(c, c).wait_recv())
    over(n_col, col, lambda c: from_col_of(all_meta_ref, meta_send, meta_recv, c).wait_recv())
    over(n_col, col, wait_from_sibling)
    over(n_col, col, wait_to_sibling)
    over(n_col, col, lambda c: x_copy(c, high).wait_send())
    over(n_col, col, lambda c: y_copy(col, c).wait_send())
    over(n_col, col, lambda c: to_col(meta, all_meta_ref, meta_send, meta_recv, c).wait_send())
    over(n_col, col, lambda c: h_copy(col, c).wait_send())
    over(n_row, row, lambda r: g_copy(row, r).wait_send())
    local_y.wait()
    local_meta.wait()


def map_kernel(
    n_row, n_col, sb, tb, slots, width,
    meta_ref, x_ref, y_ref, lse_f_ref, all_g_ref, all_y_ref,
    f_ref, g_ref, bary_ref,
    x_aug, acc, peak, weights, work, *bufs,
):
    deep = 3 * width
    extra = depth_of(width) - deep
    col = lax.axis_index("col")
    log_ns = math.log(sb * BLOCK * n_row)
    log_nt = math.log(tb * BLOCK * n_col)

    def prepare(s, carry):
        off = pl.multiple_of(s * BLOCK, BLOCK)
        x = x_ref[:, pl.ds(off, BLOCK)]
        for k, part in enumerate(scaled_rows(x, 2.0 * log2e / (width * epsilon))):
            x_aug[s, k * width : (k + 1) * width, :] = part
        x_aug[s, deep:, :] = tail(extra, 0.0, 1.0)
        xf = x.astype(jnp.float32)
        sq = jnp.sum(xf * xf, axis=0, keepdims=True)
        lse = lse_f_ref[pl.ds(s, 1), :]
        f_ref[:, pl.ds(off, BLOCK)] = sq * (1.0 / width) - epsilon * (log_ns + lse / log2e)
        return carry

    lax.fori_loop(0, sb, prepare, 0)
    acc[...] = jnp.zeros_like(acc)
    peak[...] = jnp.full(peak.shape, very_low, jnp.float32)

    def finish_g(t, carry):
        off = pl.multiple_of(t * BLOCK, BLOCK)
        yf = y_ref[:, pl.ds(off, BLOCK)].astype(jnp.float32)
        sq = jnp.sum(yf * yf, axis=0, keepdims=True)
        lse = all_g_ref[col, pl.ds(t, 1), :]
        g_ref[:, pl.ds(off, BLOCK)] = sq * (1.0 / width) - epsilon * (log_nt + lse / log2e)
        return carry

    lax.fori_loop(0, tb, finish_g, 0)

    def list_column(c, at):
        def put(p, at):
            work[0, at] = c
            work[1, at] = meta_ref[c, 0, 2 * p]
            work[2, at] = meta_ref[c, 0, 2 * p + 1]
            return at + 1

        return lax.fori_loop(0, meta_ref[c, 0, 2 * slots], put, at)

    tiles = lax.fori_loop(0, n_col, list_column, 0)

    def place(n):
        at = jnp.minimum(n, tiles - 1)
        return work[0, at], work[1, at], work[2, at]

    def targets(c, t):
        off = pl.multiple_of(t * BLOCK, BLOCK)
        return all_y_ref[c, :, pl.ds(off, BLOCK)].astype(jnp.bfloat16)

    def put(n, buf):
        c, s, t = place(n)
        y = targets(c, t)
        w = -all_g_ref[c, pl.ds(t, 1), :]
        lhs = jnp.concatenate([y, y, y, tail(extra, 0.0, three(w))], axis=0).T
        put_scores(buf, lhs, x_aug, s)

    def use(n, buf):
        c, s, t = place(n)
        sums = jnp.concatenate([targets(c, t), jnp.ones((SUMS, BLOCK), jnp.bfloat16)], axis=0)
        for h in range(BLOCK // HALF):
            at = slice(h * HALF, (h + 1) * HALF)
            top = column_top(buf, at)
            for k in range(0, BLOCK, RUN):
                run = slice(k, k + RUN)
                weights[run, at] = jnp.exp2(buf[run, at] - top).astype(jnp.bfloat16)
            part = dot(sums, weights[:, at], 1, 0)
            top = jnp.where(n < tiles, top, very_low)
            old = peak[s, :, at]
            new = jnp.maximum(old, top)
            acc[s, :, at] = acc[s, :, at] * jnp.exp2(old - new) + part * jnp.exp2(top - new)
            peak[s, :, at] = new

    put(0, bufs[0])

    def step(q, carry):
        put(2 * q + 1, bufs[1])
        use(2 * q, bufs[0])
        put(2 * q + 2, bufs[0])
        use(2 * q + 1, bufs[1])
        return carry

    lax.fori_loop(0, (tiles + 1) // 2, step, 0)

    def finish(s, carry):
        off = pl.multiple_of(s * BLOCK, BLOCK)
        bary_ref[:, pl.ds(off, BLOCK)] = acc[s, :width, :] * (
            1.0 / acc[s, width : width + 1, :])
        return carry

    lax.fori_loop(0, sb, finish, 0)


def in_hbm(x):
    return pltpu.with_memory_space_constraint(x, pltpu.HBM)


def body(n_row, n_col, src_latent, tgt_latent, g_start, pairs, counts):
    width, src_len = src_latent.shape
    tgt_len = tgt_latent.shape[1]
    slots = pairs.shape[2]
    sb, tb = src_len // BLOCK, tgt_len // BLOCK
    rows = depth_of(width)
    sizes = (n_row, n_col, sb, tb, slots, width)
    vmem = pl.BlockSpec(memory_space=pltpu.VMEM)
    smem = pl.BlockSpec(memory_space=pltpu.SMEM)
    hbm = pl.BlockSpec(memory_space=pltpu.HBM)
    anywhere = pl.BlockSpec(memory_space=pl.ANY)
    limit = pltpu.CompilerParams
    f32 = jnp.float32
    sem = pltpu.SemaphoreType.DMA

    lse_f, all_g, all_y, all_meta = pl.pallas_call(
        functools.partial(potentials_kernel, *sizes),
        out_shape=(
            jax.ShapeDtypeStruct((sb, BLOCK), f32),
            jax.ShapeDtypeStruct((n_col, tb, BLOCK), f32),
            jax.ShapeDtypeStruct((n_col, width, tgt_len), f32),
            jax.ShapeDtypeStruct((n_col, 1, 128), jnp.int32),
        ),
        in_specs=[hbm, hbm, hbm, hbm, smem],
        out_specs=(vmem, vmem, anywhere, vmem),
        scratch_shapes=[
            pltpu.VMEM((width, src_len), jnp.bfloat16),
            pltpu.VMEM((width, tgt_len), jnp.bfloat16),
            pltpu.VMEM((1, tgt_len), f32),
            pltpu.SMEM((1, 1, 2, slots), jnp.int32),
            pltpu.VMEM((sb, rows, BLOCK), jnp.bfloat16),
            pltpu.VMEM((tb, rows, BLOCK), jnp.bfloat16),
            pltpu.VMEM((tb, BLOCK, rows), jnp.bfloat16),
            pltpu.VMEM((width, tgt_len), f32),
            pltpu.VMEM((slots, BLOCK), f32),
            pltpu.VMEM((n_col, sb, BLOCK), f32),
            pltpu.VMEM((n_row, tb, BLOCK), f32),
            pltpu.VMEM((1, 128), jnp.int32),
            sem((n_col,)), sem((n_col,)), sem((n_col,)), sem((n_col,)),
            sem((n_row,)), sem((n_row,)), sem((n_col,)), sem((n_col,)),
            sem((n_col,)), sem((n_col,)), sem((n_col,)), sem((n_col,)),
            sem((2, n_col)), sem((2, n_col)), sem((6,)),
            *[pltpu.VMEM((BLOCK, BLOCK), f32)] * math.gcd(slots, 4),
        ],
        compiler_params=limit(
            collective_id=0, has_side_effects=True, vmem_limit_bytes=32 * 2**20
        ),
    )(
        in_hbm(src_latent),
        in_hbm(tgt_latent),
        in_hbm(g_start.reshape(1, tgt_len)),
        in_hbm(pairs.transpose(0, 1, 3, 2)),
        counts,
    )

    f_new, g_new, bary = pl.pallas_call(
        functools.partial(map_kernel, *sizes),
        out_shape=(
            jax.ShapeDtypeStruct((1, src_len), f32),
            jax.ShapeDtypeStruct((1, tgt_len), f32),
            jax.ShapeDtypeStruct((width, src_len), f32),
        ),
        in_specs=[smem, vmem, vmem, vmem, vmem, vmem],
        out_specs=(vmem, vmem, vmem),
        scratch_shapes=[
            pltpu.VMEM((sb, rows, BLOCK), jnp.bfloat16),
            pltpu.VMEM((sb, width + SUMS, BLOCK), f32),
            pltpu.VMEM((sb, 1, BLOCK), f32),
            pltpu.VMEM((BLOCK, BLOCK), jnp.bfloat16),
            pltpu.SMEM((3, n_col * slots), jnp.int32),
            *[pltpu.VMEM((BLOCK, BLOCK), f32)] * 2,
        ],
        compiler_params=limit(vmem_limit_bytes=40 * 2**20),
    )(all_meta, src_latent, tgt_latent, lse_f, all_g, all_y)
    return (f_new.reshape(src_len), g_new.reshape(tgt_len), bary)


def solution(mesh):
    in_specs = (
        P(None, "row"),
        P(None, "col"),
        P("col"),
        P("row", "col", None, None),
        P("row", "col"),
    )
    out_specs = (P("row"), P("col"), P(None, "row"))
    return jax.shard_map(
        functools.partial(body, mesh.shape["row"], mesh.shape["col"]),
        mesh=mesh, in_specs=in_specs, out_specs=out_specs, check_vma=False,
    )
```

profile of v0, /device:TPU:0, one launch (start us, length us, event | category | flops | bytes accessed | tf_op | source)
XLA Modules:
  0.0 34.7 jit_solution(6589102969166740131)
XLA Ops:
  0.6 0.0 copy-start
  1.3 0.0 copy-start.1
  1.3 25.5 %shard_map.76 = (f32[8,512]{1,0:T(8,128)S(1)}, f32[4,4,512]{2,1,0:T(4,128)S(1)}, f32[4,32,2048]{2,1,0:T(8,128)S(1)}, s32[4,1,128]{2,1,0:T(1,128)S(1)}) custom-call(bf16[32,4096]{1,0:T(8,128)(2,1)} %x_ref.1, bf16[32,2048]{1,0:T(8,128)(2,1)} %y_ref.1, f32[1,2048]{1,0:T(1,128)} %bitcast.4, s32[1,1,2,8]{3,2,1,0:T(2,128)} %bitcast.5, s32[1,1]{1,0:T(1,128)S(6)} %copy.8.counts_ref), custom_call_target="tpu_custom_call" | custom-call | tf_op jit(solution)/shard_map/pallas_call | solution.py:453
  26.9 0.0 copy-done
  26.9 0.0 copy-done.1
  26.9 7.8 %shard_map.77 = (f32[1,4096]{1,0:T(1,128)}, f32[1,2048]{1,0:T(1,128)}, f32[32,4096]{1,0:T(8,128)}) custom-call(s32[4,1,128]{2,1,0:T(1,128)S(1)} %get-tuple-element.10.meta_ref, bf16[32,4096]{1,0:T(8,128)(2,1)S(1)} %copy-done, bf16[32,2048]{1,0:T(8,128)(2,1)S(1)} %copy-done.1, f32[8,512]{1,0:T(8,128)S(1)} %get-tuple-element.11.lse_f_ref, ...), custom_call_target="tpu_custom_call" | custom-call | tf_op jit(solution)/shard_map/pallas_call | solution.py:493
Async XLA Ops:
  0.6 26.3 %copy-start = (bf16[32,4096]{1,0:T(8,128)(2,1)S(1)}, bf16[32,4096]{1,0:T(8,128)(2,1)}, u32[]{:S(2)}) copy-start(bf16[32,4096]{1,0:T(8,128)(2,1)} %x_ref.1) | copy-start | bytes 786436
  1.3 25.6 %copy-start.1 = (bf16[32,2048]{1,0:T(8,128)(2,1)S(1)}, bf16[32,2048]{1,0:T(8,128)(2,1)}, u32[]{:S(2)}) copy-start(bf16[32,2048]{1,0:T(8,128)(2,1)} %y_ref.1) | copy-start | bytes 393220
where the time goes:
time: 35.3 us; the launch traced here: 34.7 us
  Pallas kernels  33.4 us (95%)
  between operations  1.36 us (4%)
    pallas_call x1, Pallas kernels, body(): pl.pallas_call(functools.partial(potentials_kernel, *sizes), out_shape=(j...  25.5 us
    pallas_call x1, Pallas kernels, body(): pl.pallas_call(functools.partial(map_kernel, *sizes), out_shape=(jax.Shap...  7.81 us

commit v1 on v0

--- a/solution.py
+++ b/solution.py
@@ -96,19 +96,25 @@
     return jnp.where(total > 0.0, top + jnp.log(jnp.maximum(total, 1e-30)) * log2e, very_low)
 
 
+def repeat(n, step, state=None):
+    if n > 8:
+        return lax.fori_loop(0, n, step, state)
+    for k in range(n):
+        state = step(k, state)
+    return state
+
+
 def merge_devices(ref, n):
-    top = lax.fori_loop(1, n, lambda c, t: jnp.maximum(t, ref[c]), ref[0])
-    total = lax.fori_loop(
-        0, n, lambda c, t: t + jnp.exp2(ref[c] - top), jnp.zeros(top.shape, jnp.float32)
-    )
+    top = repeat(n, lambda c, t: jnp.maximum(t, ref[c]), ref[0])
+    total = repeat(n, lambda c, t: t + jnp.exp2(ref[c] - top), jnp.zeros(top.shape, jnp.float32))
     return top + jnp.log(total) * log2e
 
 
 def potentials_kernel(
     n_row, n_col, sb, tb, slots, width,
     x_hbm, y_hbm, g_hbm, pairs_hbm, counts_ref,
-    lse_f_ref, all_g_ref, all_y_ref, all_meta_ref,
-    x_ref, y_ref, g_ref, pairs_ref, x_aug, y_aug, y_flip, y_wide, slot_lse, from_col, from_row, meta,
+    f_rows, g_rows, x_aug, all_g_ref, all_y_ref, all_meta_ref,
+    x_ref, y_ref, g_ref, pairs_ref, lse_f_ref, sq_x, sq_y, y_aug, y_flip, y_wide, slot_lse, from_col, from_row, meta,
     meta_send, meta_recv, f_send, f_recv, g_send, g_recv, h_send, h_recv,
     y_send, y_recv, x_send, x_recv, z_send, z_recv, local_sem, *bufs,
 ):
@@ -177,29 +183,36 @@
     meta[...] = packed
 
     def prepare_x(s, carry):
-        off = pl.multiple_of(s * BLOCK, BLOCK)
-        x = x_ref[:, pl.ds(off, BLOCK)]
+        x = x_ref[:, s * BLOCK : (s + 1) * BLOCK]
         for k, part in enumerate(scaled_rows(x, 2.0 * log2e / (width * epsilon))):
             x_aug[s, k * width : (k + 1) * width, :] = part
         x_aug[s, deep:, :] = tail(extra, 0.0, 1.0)
+        xf = x.astype(jnp.float32)
+        sq_x[s : s + 1, :] = jnp.sum(xf * xf, axis=0, keepdims=True) * (1.0 / width)
         return carry
 
     def prepare_y(t, carry):
-        off = pl.multiple_of(t * BLOCK, BLOCK)
-        y = y_ref[:, pl.ds(off, BLOCK)]
+        at = slice(t * BLOCK, (t + 1) * BLOCK)
+        y = y_ref[:, at]
         yf = y.astype(jnp.float32)
-        y_wide[:, pl.ds(off, BLOCK)] = yf
+        y_wide[:, at] = yf
         for k in range(3):
             y_aug[t, k * width : (k + 1) * width, :] = y
-        sq = jnp.sum(yf * yf, axis=0, keepdims=True)
-        v = (g_ref[:, pl.ds(off, BLOCK)] - sq * (1.0 / width)) * (log2e / epsilon)
+        sq = jnp.sum(yf * yf, axis=0, keepdims=True) * (1.0 / width)
+        sq_y[t : t + 1, :] = sq
+        v = (g_ref[:, at] - sq) * (log2e / epsilon)
         y_aug[t, deep:, :] = tail(extra, 1.0, three(v))
         y_flip[t] = y_aug[t].T
         return carry
 
     get_y.wait()
     get_g.wait()
-    lax.fori_loop(0, tb, prepare_y, 0)
+    for t in range(tb):
+        prepare_y(t, 0)
+    get_x.wait()
+    for s in range(sb):
+        prepare_x(s, 0)
+
     def y_copy(source, c):
         return pltpu.make_async_remote_copy(
             src_ref=y_wide.at[rows_of(high, low)],
@@ -215,9 +228,6 @@
     local_y.start()
     local_meta = pltpu.make_async_copy(meta, all_meta_ref.at[col], local_sem.at[1])
     local_meta.start()
-
-    get_x.wait()
-    lax.fori_loop(0, sb, prepare_x, 0)
 
     group = math.gcd(slots, 4)
 
@@ -317,6 +327,14 @@
             device_id=(row, c), device_id_type=MESH)
 
     over(n_col, col, lambda c: h_copy(col, c).start())
+
+    log_ns = math.log(sb * BLOCK * n_row)
+    log_nt = math.log(tb * BLOCK * n_col)
+    f_rows[...] = sq_x[...] - epsilon * (log_ns + lse_f_ref[...] / log2e)
+    g_rows[...] = sq_y[...] - epsilon * (log_nt + all_g_ref[col] / log2e)
+    for s in range(sb):
+        x_aug[s, deep:, :] = tail(extra, 0.0, 1.0)
+
 
     over(n_col, col, lambda c: h_copy(c, c).wait_recv())
     over(n_col, col, lambda c: from_col_of(all_meta_ref, meta_send, meta_recv, c).wait_recv())
@@ -333,41 +351,16 @@
 
 def map_kernel(
     n_row, n_col, sb, tb, slots, width,
-    meta_ref, x_ref, y_ref, lse_f_ref, all_g_ref, all_y_ref,
+    meta_ref, f_rows, g_rows, x_aug, all_g_ref, all_y_ref,
     f_ref, g_ref, bary_ref,
-    x_aug, acc, peak, weights, work, *bufs,
+    acc, peak, weights, work, *bufs,
 ):
-    deep = 3 * width
-    extra = depth_of(width) - deep
-    col = lax.axis_index("col")
-    log_ns = math.log(sb * BLOCK * n_row)
-    log_nt = math.log(tb * BLOCK * n_col)
-
-    def prepare(s, carry):
-        off = pl.multiple_of(s * BLOCK, BLOCK)
-        x = x_ref[:, pl.ds(off, BLOCK)]
-        for k, part in enumerate(scaled_rows(x, 2.0 * log2e / (width * epsilon))):
-            x_aug[s, k * width : (k + 1) * width, :] = part
-        x_aug[s, deep:, :] = tail(extra, 0.0, 1.0)
-        xf = x.astype(jnp.float32)
-        sq = jnp.sum(xf * xf, axis=0, keepdims=True)
-        lse = lse_f_ref[pl.ds(s, 1), :]
-        f_ref[:, pl.ds(off, BLOCK)] = sq * (1.0 / width) - epsilon * (log_ns + lse / log2e)
-        return carry
-
-    lax.fori_loop(0, sb, prepare, 0)
+    extra = depth_of(width) - 3 * width
+    for rows, out, n in ((f_rows, f_ref, sb), (g_rows, g_ref, tb)):
+        for k in range(n):
+            out[:, k * BLOCK : (k + 1) * BLOCK] = rows[k : k + 1, :]
     acc[...] = jnp.zeros_like(acc)
     peak[...] = jnp.full(peak.shape, very_low, jnp.float32)
-
-    def finish_g(t, carry):
-        off = pl.multiple_of(t * BLOCK, BLOCK)
-        yf = y_ref[:, pl.ds(off, BLOCK)].astype(jnp.float32)
-        sq = jnp.sum(yf * yf, axis=0, keepdims=True)
-        lse = all_g_ref[col, pl.ds(t, 1), :]
-        g_ref[:, pl.ds(off, BLOCK)] = sq * (1.0 / width) - epsilon * (log_nt + lse / log2e)
-        return carry
-
-    lax.fori_loop(0, tb, finish_g, 0)
 
     def list_column(c, at):
         def put(p, at):
@@ -422,13 +415,9 @@
 
     lax.fori_loop(0, (tiles + 1) // 2, step, 0)
 
-    def finish(s, carry):
-        off = pl.multiple_of(s * BLOCK, BLOCK)
-        bary_ref[:, pl.ds(off, BLOCK)] = acc[s, :width, :] * (
+    for s in range(sb):
+        bary_ref[:, s * BLOCK : (s + 1) * BLOCK] = acc[s, :width, :] * (
             1.0 / acc[s, width : width + 1, :])
-        return carry
-
-    lax.fori_loop(0, sb, finish, 0)
 
 
 def in_hbm(x):
@@ -450,22 +439,26 @@
     f32 = jnp.float32
     sem = pltpu.SemaphoreType.DMA
 
-    lse_f, all_g, all_y, all_meta = pl.pallas_call(
+    f_rows, g_rows, x_aug, all_g, all_y, all_meta = pl.pallas_call(
         functools.partial(potentials_kernel, *sizes),
         out_shape=(
             jax.ShapeDtypeStruct((sb, BLOCK), f32),
+            jax.ShapeDtypeStruct((tb, BLOCK), f32),
+            jax.ShapeDtypeStruct((sb, rows, BLOCK), jnp.bfloat16),
             jax.ShapeDtypeStruct((n_col, tb, BLOCK), f32),
             jax.ShapeDtypeStruct((n_col, width, tgt_len), f32),
             jax.ShapeDtypeStruct((n_col, 1, 128), jnp.int32),
         ),
         in_specs=[hbm, hbm, hbm, hbm, smem],
-        out_specs=(vmem, vmem, anywhere, vmem),
+        out_specs=(vmem, vmem, vmem, vmem, anywhere, vmem),
         scratch_shapes=[
             pltpu.VMEM((width, src_len), jnp.bfloat16),
             pltpu.VMEM((width, tgt_len), jnp.bfloat16),
             pltpu.VMEM((1, tgt_len), f32),
             pltpu.SMEM((1, 1, 2, slots), jnp.int32),
-            pltpu.VMEM((sb, rows, BLOCK), jnp.bfloat16),
+            pltpu.VMEM((sb, BLOCK), f32),
+            pltpu.VMEM((sb, BLOCK), f32),
+            pltpu.VMEM((tb, BLOCK), f32),
             pltpu.VMEM((tb, rows, BLOCK), jnp.bfloat16),
             pltpu.VMEM((tb, BLOCK, rows), jnp.bfloat16),
             pltpu.VMEM((width, tgt_len), f32),
@@ -500,7 +493,6 @@
         in_specs=[smem, vmem, vmem, vmem, vmem, vmem],
         out_specs=(vmem, vmem, vmem),
         scratch_shapes=[
-            pltpu.VMEM((sb, rows, BLOCK), jnp.bfloat16),
             pltpu.VMEM((sb, width + SUMS, BLOCK), f32),
             pltpu.VMEM((sb, 1, BLOCK), f32),
             pltpu.VMEM((BLOCK, BLOCK), jnp.bfloat16),
@@ -508,7 +500,7 @@
             *[pltpu.VMEM((BLOCK, BLOCK), f32)] * 2,
         ],
         compiler_params=limit(vmem_limit_bytes=40 * 2**20),
-    )(all_meta, src_latent, tgt_latent, lse_f, all_g, all_y)
+    )(all_meta, f_rows, g_rows, x_aug, all_g, all_y)
     return (f_new.reshape(src_len), g_new.reshape(tgt_len), bary)
 
 

time: 35.3 us -> 35.5 us (level)
    pallas_call x1, Pallas kernels: 7.81 us -> 8.27 us  [body(): pl.pallas_call(functools.partial(map_kernel, *sizes), out_shape=(jax.Shap...]
where the time goes in v1:
time: 35.5 us; the launch traced here: 34.9 us
  Pallas kernels  33.6 us (95%)
  between operations  1.29 us (4%)
    pallas_call x1, Pallas kernels, body(): pl.pallas_call(functools.partial(potentials_kernel, *sizes), out_shape=(j...  25.4 us
    pallas_call x1, Pallas kernels, body(): pl.pallas_call(functools.partial(map_kernel, *sizes), out_shape=(jax.Shap...  8.27 us

profile of v1, /device:TPU:0, one launch (start us, length us, event | category | flops | bytes accessed | tf_op | source)
XLA Modules:
  0.0 34.9 jit_solution(7015579243093195477)
XLA Ops:
  1.3 25.4 %shard_map.76 = (f32[8,512]{1,0:T(8,128)S(1)}, f32[4,512]{1,0:T(4,128)S(1)}, bf16[8,128,512]{2,1,0:T(8,128)(2,1)S(1)}, f32[4,4,512]{2,1,0:T(4,128)S(1)}, f32[4,3...) custom-call(bf16[32,4096]{1,0:T(8,128)(2,1)} %x_hbm.1, bf16[32,2048]{1,0:T(8,128)(2,1)} %y_hbm.1, f32[1,2048]{1,0:T(1,128)} %bitcast.4, ...), custom_call_target="tpu_custom_call" | custom-call | tf_op jit(solution)/shard_map/pallas_call | solution.py:442
  26.7 8.3 %shard_map.77 = (f32[1,4096]{1,0:T(1,128)}, f32[1,2048]{1,0:T(1,128)}, f32[32,4096]{1,0:T(8,128)}) custom-call(s32[4,1,128]{2,1,0:T(1,128)S(1)} %get-tuple-element.12.meta_ref, f32[8,512]{1,0:T(8,128)S(1)} %get-tuple-element.13.f_rows, f32[4,512]{1,0:T(4,128)S(1)} %get-tuple-element.14.g_rows, bf16[8,128,512]{2,1,0:T(8,128)(2,1)S(1)} %get-tuple-element.15.x_aug, ...), custom_call_target="tpu_custom_call" | custom-call | tf_op jit(solution)/shard_map/pallas_call | solution.py:486

commit v2 on v1

--- a/solution.py
+++ b/solution.py
@@ -114,7 +114,7 @@
     n_row, n_col, sb, tb, slots, width,
     x_hbm, y_hbm, g_hbm, pairs_hbm, counts_ref,
     f_rows, g_rows, x_aug, all_g_ref, all_y_ref, all_meta_ref,
-    x_ref, y_ref, g_ref, pairs_ref, lse_f_ref, sq_x, sq_y, y_aug, y_flip, y_wide, slot_lse, from_col, from_row, meta,
+    x_ref, y_ref, g_ref, pairs_ref, lse_f_ref, merged_f, sq_x, sq_y, y_aug, y_flip, y_wide, slot_lse, from_col, from_row, meta,
     meta_send, meta_recv, f_send, f_recv, g_send, g_recv, h_send, h_recv,
     y_send, y_recv, x_send, x_recv, z_send, z_recv, local_sem, *bufs,
 ):
@@ -229,7 +229,7 @@
     local_meta = pltpu.make_async_copy(meta, all_meta_ref.at[col], local_sem.at[1])
     local_meta.start()
 
-    group = math.gcd(slots, 4)
+    group = math.gcd(slots, 8)
 
     def in_turn(put, q):
         put(0)
@@ -253,7 +253,6 @@
     from_col[col] = lse_f_ref[...]
 
     over(n_col, col, lambda c: to_col(lse_f_ref, from_col, f_send, f_recv, c).start())
-    over(n_col, col, lambda c: from_col_of(from_col, f_send, f_recv, c).wait_recv())
 
     def x_copy(source, high):
         return pltpu.make_async_remote_copy(
@@ -267,10 +266,10 @@
         x_copy(c, high).start()
 
     over(n_col, col, pass_across)
-    over(n_col, col, lambda c: to_col(lse_f_ref, from_col, f_send, f_recv, c).wait_send())
+    over(n_col, col, lambda c: from_col_of(from_col, f_send, f_recv, c).wait_recv())
 
     merged = merge_devices(from_col, n_col)
-    lse_f_ref[...] = merged
+    merged_f[...] = merged
     for s in range(sb):
         u = -math.log2(sb * BLOCK * n_row) - merged[s : s + 1, :]
         x_aug[s, deep:, :] = tail(extra, three(u), 0.0)
@@ -330,23 +329,24 @@
 
     log_ns = math.log(sb * BLOCK * n_row)
     log_nt = math.log(tb * BLOCK * n_col)
-    f_rows[...] = sq_x[...] - epsilon * (log_ns + lse_f_ref[...] / log2e)
+    f_rows[...] = sq_x[...] - epsilon * (log_ns + merged_f[...] / log2e)
     g_rows[...] = sq_y[...] - epsilon * (log_nt + all_g_ref[col] / log2e)
     for s in range(sb):
         x_aug[s, deep:, :] = tail(extra, 0.0, 1.0)
 
 
-    over(n_col, col, lambda c: h_copy(c, c).wait_recv())
-    over(n_col, col, lambda c: from_col_of(all_meta_ref, meta_send, meta_recv, c).wait_recv())
-    over(n_col, col, wait_from_sibling)
-    over(n_col, col, wait_to_sibling)
-    over(n_col, col, lambda c: x_copy(c, high).wait_send())
+    over(n_col, col, lambda c: to_col(lse_f_ref, from_col, f_send, f_recv, c).wait_send())
     over(n_col, col, lambda c: y_copy(col, c).wait_send())
     over(n_col, col, lambda c: to_col(meta, all_meta_ref, meta_send, meta_recv, c).wait_send())
-    over(n_col, col, lambda c: h_copy(col, c).wait_send())
+    over(n_col, col, lambda c: from_col_of(all_meta_ref, meta_send, meta_recv, c).wait_recv())
+    over(n_col, col, lambda c: x_copy(c, high).wait_send())
     over(n_row, row, lambda r: g_copy(row, r).wait_send())
     local_y.wait()
     local_meta.wait()
+    over(n_col, col, wait_from_sibling)
+    over(n_col, col, wait_to_sibling)
+    over(n_col, col, lambda c: h_copy(col, c).wait_send())
+    over(n_col, col, lambda c: h_copy(c, c).wait_recv())
 
 
 def map_kernel(
@@ -406,14 +406,21 @@
 
     put(0, bufs[0])
 
-    def step(q, carry):
-        put(2 * q + 1, bufs[1])
-        use(2 * q, bufs[0])
-        put(2 * q + 2, bufs[0])
-        use(2 * q + 1, bufs[1])
-        return carry
-
-    lax.fori_loop(0, (tiles + 1) // 2, step, 0)
+    def run(first, steps, pairs):
+        def step(q, carry):
+            for k in range(pairs):
+                n = first + 2 * (q * pairs + k)
+                put(n + 1, bufs[1])
+                use(n, bufs[0])
+                put(n + 2, bufs[0])
+                use(n + 1, bufs[1])
+            return carry
+
+        lax.fori_loop(0, steps, step, 0)
+
+    fours = tiles // 4
+    run(0, fours, 2)
+    run(4 * fours, (tiles - 4 * fours + 1) // 2, 1)
 
     for s in range(sb):
         bary_ref[:, s * BLOCK : (s + 1) * BLOCK] = acc[s, :width, :] * (
@@ -458,6 +465,7 @@
             pltpu.SMEM((1, 1, 2, slots), jnp.int32),
             pltpu.VMEM((sb, BLOCK), f32),
             pltpu.VMEM((sb, BLOCK), f32),
+            pltpu.VMEM((sb, BLOCK), f32),
             pltpu.VMEM((tb, BLOCK), f32),
             pltpu.VMEM((tb, rows, BLOCK), jnp.bfloat16),
             pltpu.VMEM((tb, BLOCK, rows), jnp.bfloat16),
@@ -470,7 +478,7 @@
             sem((n_row,)), sem((n_row,)), sem((n_col,)), sem((n_col,)),
             sem((n_col,)), sem((n_col,)), sem((n_col,)), sem((n_col,)),
             sem((2, n_col)), sem((2, n_col)), sem((6,)),
-            *[pltpu.VMEM((BLOCK, BLOCK), f32)] * math.gcd(slots, 4),
+            *[pltpu.VMEM((BLOCK, BLOCK), f32)] * math.gcd(slots, 8),
         ],
         compiler_params=limit(
             collective_id=0, has_side_effects=True, vmem_limit_bytes=32 * 2**20

time: 35.5 us -> 34.8 us (0.980); the launches traced: 34.9 us -> 34.6 us
    pallas_call x1, Pallas kernels: 25.4 us -> 24.8 us  [body(): pl.pallas_call(functools.partial(potentials_kernel, *sizes), out_shape=(j...]
where the time goes in v2:
time: 34.8 us; the launch traced here: 34.6 us
  Pallas kernels  33.3 us (96%)
  between operations  1.29 us (4%)
    pallas_call x1, Pallas kernels, body(): pl.pallas_call(functools.partial(potentials_kernel, *sizes), out_shape=(j...  24.8 us
    pallas_call x1, Pallas kernels, body(): pl.pallas_call(functools.partial(map_kernel, *sizes), out_shape=(jax.Shap...  8.54 us

profile of v2, /device:TPU:0, one launch (start us, length us, event | category | flops | bytes accessed | tf_op | source)
XLA Modules:
  0.0 34.6 jit_solution(17590243927523995018)
XLA Ops:
  1.3 24.8 %shard_map.76 = (f32[8,512]{1,0:T(8,128)S(1)}, f32[4,512]{1,0:T(4,128)S(1)}, bf16[8,128,512]{2,1,0:T(8,128)(2,1)S(1)}, f32[4,4,512]{2,1,0:T(4,128)S(1)}, f32[4,3...) custom-call(bf16[32,4096]{1,0:T(8,128)(2,1)} %x_hbm.1, bf16[32,2048]{1,0:T(8,128)(2,1)} %y_hbm.1, f32[1,2048]{1,0:T(1,128)} %bitcast.4, ...), custom_call_target="tpu_custom_call" | custom-call | tf_op jit(solution)/shard_map/pallas_call | solution.py:449
  26.1 8.5 %shard_map.77 = (f32[1,4096]{1,0:T(1,128)}, f32[1,2048]{1,0:T(1,128)}, f32[32,4096]{1,0:T(8,128)}) custom-call(s32[4,1,128]{2,1,0:T(1,128)S(1)} %get-tuple-element.12.meta_ref, f32[8,512]{1,0:T(8,128)S(1)} %get-tuple-element.13.f_rows, f32[4,512]{1,0:T(4,128)S(1)} %get-tuple-element.14.g_rows, bf16[8,128,512]{2,1,0:T(8,128)(2,1)S(1)} %get-tuple-element.15.x_aug, ...), custom_call_target="tpu_custom_call" | custom-call | tf_op jit(solution)/shard_map/pallas_call | solution.py:494
